TPU v7x, 32 devices: a whole 2x2x4 slice. The times are simulated.
32 devices in a mesh: groups: 2 (over x), blocks: 16 (over z, y, core).
Axes of the slice: x: 2, y: 2, z: 4, core: 2. Of those that a mesh axis runs over, the one named last changes fastest.
Arguments:
- probes: bfloat16 [8192, 256], P(('groups', 'blocks')), parts along dimension 0, may hold values from -4 to 4
- cheb_coef: float32 [10], P('groups'), parts along dimension 0, may hold values from 0.5 to 1.5
- col_basis: bfloat16 [8192, 64], P(('groups', 'blocks')), parts along dimension 0, may hold values from -0.375 to 0.375
- row_basis: bfloat16 [8192, 64], P(('groups', 'blocks')), parts along dimension 0, may hold values from -0.0234375 to 0.0234375
- near_tiles: bfloat16 [8192, 768], P(('groups', 'blocks')), parts along dimension 0, may hold values from -0.0546875 to 0.0546875
- coupling: bfloat16 [2048, 64, 64], P(('groups', 'blocks')), parts along dimension 0, may hold values from -0.75 to 0.75
- far_rows: int32 [2048, 1], P(('groups', 'blocks')), parts along dimension 0, may hold values from 0 to 15; in each aligned block of 64 rows (0 to 63, 64 to 127, ...) at most 8 rows name the same one
- far_cols: int32 [2048], P(('groups', 'blocks')), parts along dimension 0, may hold values from 0 to 15
Outputs:
- estimate: float32 [8192, 256], P(('groups', 'blocks')), parts along dimension 0
There are 2 independent parts, one for each index of `groups`. A program takes and returns all parts, laid end to end along the dimension named above; each array names one. Nothing has to cross between parts.
Inputs may be any that keep to these rules, and one draw needn't show every extreme that they name: `far_rows`: cluster r is the rows r * 256 onward. Among the 64 coupling blocks of one device at most 8 share a row cluster, and that many do on some device.
All inputs are finite; a program needn't handle non-finite values.
Results may differ from a plain program's by a relative error of at most 0.0085.
Values may be sent and summed in bfloat16 or wider, within the bound.
A program may use at most 64 MiB of HBM per device.

v0:
```python
import jax
import jax.numpy as jnp
from jax import lax
from jax.sharding import PartitionSpec as P

ITERS = 4


def padded_2(cells, sides, width):
    for axis, dim in sides:
        count = lax.axis_size(axis)
        ends = count - 1
        head = lax.slice_in_dim(cells, 0, width, axis=dim)
        tail = lax.slice_in_dim(cells, cells.shape[dim] - width, cells.shape[dim], axis=dim)
        cells = jnp.concatenate(
            [
                lax.ppermute(tail, axis, [(i, (i + 1) % count) for i in range(ends)]),
                cells,
                lax.ppermute(head, axis, [((i + 1) % count, i) for i in range(ends)]),
            ],
            axis=dim,
        )
    return cells


def shards(probes, cheb_coef, col_basis, row_basis, near_tiles, coupling, far_rows, far_cols):
    leaf_count = coupling.shape[0]
    rank_size = coupling.shape[1]
    cluster_rows = probes.shape[0]
    probe_count = probes.shape[1]
    device_count = lax.axis_size("blocks")
    row_ids = far_rows[:, 0]
    row_pick = (row_ids[None, :] == jnp.arange(device_count, dtype=jnp.int32)[:, None]).astype(
        jnp.bfloat16
    )
    t_now = probes.astype(jnp.float32)
    t_prev = jnp.zeros_like(t_now)
    estimate = cheb_coef[0] * t_now
    for turn in range(ITERS):
        current = t_now.astype(jnp.bfloat16)
        moments = lax.dot_general(
            col_basis, current, (((0,), (0,)), ((), ())), preferred_element_type=jnp.float32
        ).astype(jnp.bfloat16)
        flat_moments = moments.reshape(1, rank_size * probe_count)
        piece = lax.all_gather(flat_moments, "blocks", axis=0, tiled=True)
        chosen = (far_cols[:, None] == jnp.arange(piece.shape[0], dtype=jnp.int32)[None, :]).astype(
            jnp.bfloat16
        )
        selected = jnp.dot(chosen, piece, preferred_element_type=jnp.float32).astype(jnp.bfloat16)
        selected_blocks = selected.reshape(leaf_count, rank_size, probe_count)
        terms = jnp.einsum(
            "lij,ljp->lip", coupling, selected_blocks, preferred_element_type=jnp.float32
        )
        terms = terms.reshape(leaf_count, rank_size * probe_count)
        upper_part = terms.astype(jnp.bfloat16)
        lower_part = (terms - upper_part.astype(jnp.float32)).astype(jnp.bfloat16)
        table = jnp.dot(row_pick, upper_part, preferred_element_type=jnp.float32) + jnp.dot(
            row_pick, lower_part, preferred_element_type=jnp.float32
        )
        received = lax.all_to_all(
            table.astype(jnp.bfloat16), "blocks", split_axis=0, concat_axis=0, tiled=True
        ).astype(table.dtype)
        far_sum = jnp.sum(received, axis=0).reshape(rank_size, probe_count)
        far_rounded = far_sum.astype(jnp.bfloat16)
        padded = padded_2(current, (("blocks", 0),), cluster_rows)
        near = jnp.dot(near_tiles, padded, preferred_element_type=jnp.float32)
        image = near + jnp.dot(row_basis, far_rounded, preferred_element_type=jnp.float32)
        if turn == 0:
            t_next = image
        else:
            t_next = 2.0 * image - t_prev
        estimate = estimate + cheb_coef[turn + 1] * t_next
        t_prev = t_now
        t_now = t_next
    return estimate


def solution(mesh):
    return jax.shard_map(
        shards,
        mesh=mesh,
        in_specs=(
            P(("groups", "blocks"), None),
            P("groups"),
            P(("groups", "blocks"), None),
            P(("groups", "blocks"), None),
            P(("groups", "blocks"), None),
            P(("groups", "blocks"), None, None),
            P(("groups", "blocks"), None),
            P(("groups", "blocks")),
        ),
        out_specs=P(("groups", "blocks"), None),
        check_vma=False,
    )
```

profile of v0, /device:TPU:0, one launch (start us, length us, event | category | flops | bytes accessed | tf_op | source)
XLA Modules:
  0.0 219.3 jit_solution(11088170286344567645)
XLA Ops:
  0.0 1.1 convolution_convert_fusion.7
  1.2 26.2 %all-gather = bf16[16,1,16384]{2,1,0:T(2,128)(2,1)S(1)} all-gather(bf16[1,1,16384]{2,1,0:T(2,128)(2,1)S(1)} %reshape.70), channel_id=1, replica_groups=mesh['groups'=2,'blocks'=16] {'blocks'}, dimensions={0}, use_global_device_ids=true | all-gather | bytes 557056 | tf_op jit(solution)/shard_map/all_gather | solution.py:45
  27.4 1.5 convolution_convert_fusion.3
  29.5 0.7 fusion.88
  30.2 2.4 %copy.30 = f32[8,8,64,256]{3,1,2,0:T(8,128)S(1)} copy(f32[8,8,64,256]{3,2,1,0:T(8,128)S(1)} %bitcast.106) | data formatting | bytes 8388608
  33.9 0.9 reduce.8
  34.8 1.2 reshape.82
  36.0 3.7 %all-to-all-start = ((bf16[16,2,8192]{2,1,0:T(2,128)(2,1)}), bf16[16,2,8192]{2,1,0:T(2,128)(2,1)S(1)}, u32[]{:S(2)}, u32[]{:S(2)}) async-start(bf16[16,2,8192]{2,1,0:T(2,128)(2,1)} %reshape.82), calls=%async_computation | async-start | bytes 1048576 | tf_op jit(solution)/shard_map/all_to_all | solution.py:60
  39.8 1.3 collective-permute-start.1
  41.1 3.7 %collective-permute-start = (bf16[256,256]{1,0:T(8,128)(2,1)S(1)}, bf16[256,256]{1,0:T(8,128)(2,1)}, u32[]{:S(2)}, u32[]{:S(2)}) collective-permute-start(bf16[256,256]{1,0:T(8,128)(2,1)S(1)} %copy-done.3), channel_id=1, source_target_pairs={{0,1},{1,2},{2,3},{3,4},{4,5},{5,6},{6,7},{7,8},{8,9},{9,10},{10,1... | collective-permute-start | bytes 393224 | tf_op jit(solution)/shard_map/ppermute | solution.py:17
  44.7 9.4 %all-to-all-done = bf16[16,2,8192]{2,1,0:T(2,128)(2,1)S(1)} async-done(((bf16[16,2,8192]{2,1,0:T(2,128)(2,1)}), bf16[16,2,8192]{2,1,0:T(2,128)(2,1)S(1)}, u32[]{:S(2)}, u32[]{:S(2)}) %all-to-all-start) | async-done | bytes 524320 | tf_op jit(solution)/shard_map/all_to_all | solution.py:60
  54.7 1.1 reduce_sum.48
  56.7 1.2 convolution_add_fusion.7
  58.1 23.1 %all-gather.1 = bf16[16,1,16384]{2,1,0:T(2,128)(2,1)S(1)} all-gather(bf16[1,1,16384]{2,1,0:T(2,128)(2,1)S(1)} %reshape.72), channel_id=1, replica_groups=mesh['groups'=2,'blocks'=16] {'blocks'}, dimensions={0}, use_global_device_ids=true | all-gather | bytes 557056 | tf_op jit(solution)/shard_map/all_gather | solution.py:45
  81.3 0.8 convolution_convert_fusion.2
  82.7 0.7 fusion.89
  83.4 2.4 %copy.32 = f32[8,8,64,256]{3,1,2,0:T(8,128)S(1)} copy(f32[8,8,64,256]{3,2,1,0:T(8,128)S(1)} %bitcast.107) | data formatting | bytes 8388608
  86.6 0.9 reduce.9
  87.5 1.2 reshape.84
  88.7 3.6 %all-to-all-start.1 = ((bf16[16,2,8192]{2,1,0:T(2,128)(2,1)}), bf16[16,2,8192]{2,1,0:T(2,128)(2,1)S(1)}, u32[]{:S(2)}, u32[]{:S(2)}) async-start(bf16[16,2,8192]{2,1,0:T(2,128)(2,1)} %reshape.84), calls=%async_computation.1 | async-start | bytes 1048576 | tf_op jit(solution)/shard_map/all_to_all | solution.py:60
  92.3 1.3 collective-permute-start.3
  93.6 3.0 %collective-permute-start.2 = (bf16[256,256]{1,0:T(8,128)(2,1)S(1)}, bf16[256,256]{1,0:T(8,128)(2,1)S(1)}, u32[]{:S(2)}, u32[]{:S(2)}) collective-permute-start(bf16[256,256]{1,0:T(8,128)(2,1)S(1)} %convert_bitcast_fusion.1), channel_id=1, source_target_pairs={{0,1},{1,2},{2,3},{3,4},{4,5},{5,6},{6,7},{7,8},{8,9},{9,10},{10,1... | collective-permute-start | bytes 393224 | tf_op jit(solution)/shard_map/ppermute | solution.py:17
  96.6 10.1 %all-to-all-done.1 = bf16[16,2,8192]{2,1,0:T(2,128)(2,1)S(1)} async-done(((bf16[16,2,8192]{2,1,0:T(2,128)(2,1)}), bf16[16,2,8192]{2,1,0:T(2,128)(2,1)S(1)}, u32[]{:S(2)}, u32[]{:S(2)}) %all-to-all-start.1) | async-done | bytes 524320 | tf_op jit(solution)/shard_map/all_to_all | solution.py:60
  107.2 1.1 reduce_sum.49
  108.5 2.0 fusion.83
  110.7 23.2 %all-gather.2 = bf16[16,1,16384]{2,1,0:T(2,128)(2,1)S(1)} all-gather(bf16[1,1,16384]{2,1,0:T(2,128)(2,1)S(1)} %reshape.74), channel_id=1, replica_groups=mesh['groups'=2,'blocks'=16] {'blocks'}, dimensions={0}, use_global_device_ids=true | all-gather | bytes 557056 | tf_op jit(solution)/shard_map/all_gather | solution.py:45
  133.9 0.8 convolution_convert_fusion.1
  135.3 0.7 fusion.90
  136.0 2.4 %copy.34 = f32[8,8,64,256]{3,1,2,0:T(8,128)S(1)} copy(f32[8,8,64,256]{3,2,1,0:T(8,128)S(1)} %bitcast.108) | data formatting | bytes 8388608
  139.2 1.0 reduce.10
  140.1 1.2 reshape.86
  141.3 3.6 %all-to-all-start.2 = ((bf16[16,2,8192]{2,1,0:T(2,128)(2,1)}), bf16[16,2,8192]{2,1,0:T(2,128)(2,1)S(1)}, u32[]{:S(2)}, u32[]{:S(2)}) async-start(bf16[16,2,8192]{2,1,0:T(2,128)(2,1)} %reshape.86), calls=%async_computation.2 | async-start | bytes 1048576 | tf_op jit(solution)/shard_map/all_to_all | solution.py:60
  144.9 1.3 collective-permute-start.5
  146.2 3.7 %collective-permute-start.4 = (bf16[256,256]{1,0:T(8,128)(2,1)S(1)}, bf16[256,256]{1,0:T(8,128)(2,1)}, u32[]{:S(2)}, u32[]{:S(2)}) collective-permute-start(bf16[256,256]{1,0:T(8,128)(2,1)S(1)} %copy-done.5), channel_id=1, source_target_pairs={{0,1},{1,2},{2,3},{3,4},{4,5},{5,6},{6,7},{7,8},{8,9},{9,10},{10,1... | collective-permute-start | bytes 393224 | tf_op jit(solution)/shard_map/ppermute | solution.py:17
  149.9 9.4 %all-to-all-done.2 = bf16[16,2,8192]{2,1,0:T(2,128)(2,1)S(1)} async-done(((bf16[16,2,8192]{2,1,0:T(2,128)(2,1)}), bf16[16,2,8192]{2,1,0:T(2,128)(2,1)S(1)}, u32[]{:S(2)}, u32[]{:S(2)}) %all-to-all-start.2) | async-done | bytes 524320 | tf_op jit(solution)/shard_map/all_to_all | solution.py:60
  159.8 1.1 reduce_sum.50
  161.8 1.4 fusion.16
  163.4 23.2 %all-gather.3 = bf16[16,1,16384]{2,1,0:T(2,128)(2,1)S(1)} all-gather(bf16[1,1,16384]{2,1,0:T(2,128)(2,1)S(1)} %reshape.76), channel_id=1, replica_groups=mesh['groups'=2,'blocks'=16] {'blocks'}, dimensions={0}, use_global_device_ids=true | all-gather | bytes 557056 | tf_op jit(solution)/shard_map/all_gather | solution.py:45
  186.6 0.8 convolution_convert_fusion
  188.7 2.4 %copy.36 = f32[8,8,64,256]{3,1,2,0:T(8,128)S(1)} copy(f32[8,8,64,256]{3,2,1,0:T(8,128)S(1)} %bitcast.109) | data formatting | bytes 8388608
  191.9 0.9 reduce.11
  192.8 1.2 reshape.88
  194.0 3.6 %all-to-all-start.3 = ((bf16[16,2,8192]{2,1,0:T(2,128)(2,1)}), bf16[16,2,8192]{2,1,0:T(2,128)(2,1)S(1)}, u32[]{:S(2)}, u32[]{:S(2)}) async-start(bf16[16,2,8192]{2,1,0:T(2,128)(2,1)} %reshape.88), calls=%async_computation.3 | async-start | bytes 1048576 | tf_op jit(solution)/shard_map/all_to_all | solution.py:60
  198.3 1.3 collective-permute-start.7
  199.6 3.7 %collective-permute-start.6 = (bf16[256,256]{1,0:T(8,128)(2,1)S(1)}, bf16[256,256]{1,0:T(8,128)(2,1)}, u32[]{:S(2)}, u32[]{:S(2)}) collective-permute-start(bf16[256,256]{1,0:T(8,128)(2,1)S(1)} %convert_bitcast_fusion), channel_id=1, source_target_pairs={{0,1},{1,2},{2,3},{3,4},{4,5},{5,6},{6,7},{7,8},{8,9},{9,10},{10,1... | collective-permute-start | bytes 393224 | tf_op jit(solution)/shard_map/ppermute | solution.py:17
  203.3 8.8 %all-to-all-done.3 = bf16[16,2,8192]{2,1,0:T(2,128)(2,1)S(1)} async-done(((bf16[16,2,8192]{2,1,0:T(2,128)(2,1)}), bf16[16,2,8192]{2,1,0:T(2,128)(2,1)S(1)}, u32[]{:S(2)}, u32[]{:S(2)}) %all-to-all-start.3) | async-done | bytes 524320 | tf_op jit(solution)/shard_map/all_to_all | solution.py:60
  212.5 1.1 reduce_sum.51
  213.9 5.4 %fusion.15 = f32[256,256]{1,0:T(8,128)} fusion(f32[256,256]{1,0:T(8,128)} %get-tuple-element.11, f32[256,256]{0,1:T(8,128)S(1)} %fusion.87, bf16[256,768]{1,0:T(8,128)(2,1)} %param.12, bf16[256,256]{1,0:T(8,128)(2,1)} %collective-permute-done.7, bf16[256,256]{1,0:T(8,128)(2,1)S(1)} %convert_bitcast_fusion, bf16[256,256]{1,0:T(8,128)(2,1)} %collective-permute-done.6, ...), kind=kOutput, calls=%fused_computation.31 | convolution fusion | flops 102694912 | bytes 2228244 | tf_op jit(solution)/shard_map/dot_general | solution.py:66
  (68 shorter events, 12.3 us)
Async XLA Ops:
  0.0 29.5 %copy-start = (bf16[64,64,64]{2,1,0:T(8,128)(2,1)S(1)}, bf16[64,64,64]{2,1,0:T(8,128)(2,1)}, u32[]{:S(2)}) copy-start(bf16[64,64,64]{2,1,0:T(8,128)(2,1)} %param.13) | copy-start | bytes 1572868
  30.2 2.4 %copy-start.6 = (s32[64,1]{0,1:T(1,128)S(1)}, s32[64,1]{0,1:T(1,128)}, u32[]{:S(2)}) copy-start(s32[64,1]{0,1:T(1,128)} %param.14) | copy-start | bytes 772
  33.4 6.3 %copy-start.3 = (bf16[256,256]{1,0:T(8,128)(2,1)S(1)}, bf16[256,256]{1,0:T(8,128)(2,1)}, u32[]{:S(2)}) copy-start(bf16[256,256]{1,0:T(8,128)(2,1)} %param.8) | copy-start | bytes 393220
  36.0 19.8 %copy-start.1 = (bf16[256,64]{0,1:T(8,128)(2,1)S(1)}, bf16[256,64]{0,1:T(8,128)(2,1)}, u32[]{:S(2)}) copy-start(bf16[256,64]{0,1:T(8,128)(2,1)} %param.11) | copy-start | bytes 98308
  36.0 20.7 %copy-start.9 = (bf16[256,768]{1,0:T(8,128)(2,1)S(1)}, bf16[256,768]{1,0:T(8,128)(2,1)}, u32[]{:S(2)}) copy-start(bf16[256,768]{1,0:T(8,128)(2,1)} %param.12) | copy-start | bytes 1179652
  36.0 18.1 %all-to-all-start = ((bf16[16,2,8192]{2,1,0:T(2,128)(2,1)}), bf16[16,2,8192]{2,1,0:T(2,128)(2,1)S(1)}, u32[]{:S(2)}, u32[]{:S(2)}) async-start(bf16[16,2,8192]{2,1,0:T(2,128)(2,1)} %reshape.82), calls=%async_computation | async-start | bytes 1048576 | tf_op jit(solution)/shard_map/all_to_all | solution.py:60
  39.7 18.2 %copy-start.2 = (bf16[256,64]{0,1:T(8,128)(2,1)S(1)}, bf16[256,64]{0,1:T(8,128)(2,1)}, u32[]{:S(2)}) copy-start(bf16[256,64]{0,1:T(8,128)(2,1)} %param.10) | copy-start | bytes 98308
  39.8 16.3 %collective-permute-start.1 = (bf16[256,256]{1,0:T(8,128)(2,1)S(1)}, bf16[256,256]{1,0:T(8,128)(2,1)S(1)}, u32[]{:S(2)}, u32[]{:S(2)}) collective-permute-start(bf16[256,256]{1,0:T(8,128)(2,1)S(1)} %copy-done.3), channel_id=1, source_target_pairs={{1,0},{2,1},{3,2},{4,3},{5,4},{6,5},{7,6},{8,7},{9,8},{10,9},{11,1... | collective-permute-start | bytes 393224 | tf_op jit(solution)/shard_map/ppermute | solution.py:19
  41.1 15.7 %collective-permute-start = (bf16[256,256]{1,0:T(8,128)(2,1)S(1)}, bf16[256,256]{1,0:T(8,128)(2,1)}, u32[]{:S(2)}, u32[]{:S(2)}) collective-permute-start(bf16[256,256]{1,0:T(8,128)(2,1)S(1)} %copy-done.3), channel_id=1, source_target_pairs={{0,1},{1,2},{2,3},{3,4},{4,5},{5,6},{6,7},{7,8},{8,9},{9,10},{10,1... | collective-permute-start | bytes 393224 | tf_op jit(solution)/shard_map/ppermute | solution.py:17
  54.7 26.6 %copy-start.8 = (s32[64]{0:T(128)S(1)}, s32[64]{0:T(128)}, u32[]{:S(2)}) copy-start(s32[64]{0:T(128)} %param.15) | copy-start | bytes 772
  56.0 0.7 copy-start.11
  88.7 18.0 %all-to-all-start.1 = ((bf16[16,2,8192]{2,1,0:T(2,128)(2,1)}), bf16[16,2,8192]{2,1,0:T(2,128)(2,1)S(1)}, u32[]{:S(2)}, u32[]{:S(2)}) async-start(bf16[16,2,8192]{2,1,0:T(2,128)(2,1)} %reshape.84), calls=%async_computation.1 | async-start | bytes 1048576 | tf_op jit(solution)/shard_map/all_to_all | solution.py:60
  92.3 16.3 %collective-permute-start.3 = (bf16[256,256]{1,0:T(8,128)(2,1)S(1)}, bf16[256,256]{1,0:T(8,128)(2,1)S(1)}, u32[]{:S(2)}, u32[]{:S(2)}) collective-permute-start(bf16[256,256]{1,0:T(8,128)(2,1)S(1)} %convert_bitcast_fusion.1), channel_id=1, source_target_pairs={{1,0},{2,1},{3,2},{4,3},{5,4},{6,5},{7,6},{8,7},{9,8},{10,9},{11,1... | collective-permute-start | bytes 393224 | tf_op jit(solution)/shard_map/ppermute | solution.py:19
  93.6 15.0 %collective-permute-start.2 = (bf16[256,256]{1,0:T(8,128)(2,1)S(1)}, bf16[256,256]{1,0:T(8,128)(2,1)S(1)}, u32[]{:S(2)}, u32[]{:S(2)}) collective-permute-start(bf16[256,256]{1,0:T(8,128)(2,1)S(1)} %convert_bitcast_fusion.1), channel_id=1, source_target_pairs={{0,1},{1,2},{2,3},{3,4},{4,5},{5,6},{6,7},{7,8},{8,9},{9,10},{10,1... | collective-permute-start | bytes 393224 | tf_op jit(solution)/shard_map/ppermute | solution.py:17
  110.5 24.7 %copy-start.4 = (bf16[256,256]{1,0:T(8,128)(2,1)}, bf16[256,256]{1,0:T(8,128)(2,1)S(1)}, u32[]{:S(2)}) copy-start(bf16[256,256]{1,0:T(8,128)(2,1)S(1)} %get-tuple-element.10) | copy-start | bytes 393220
  139.2 5.7 %copy-start.5 = (bf16[256,256]{1,0:T(8,128)(2,1)S(1)}, bf16[256,256]{1,0:T(8,128)(2,1)}, u32[]{:S(2)}) copy-start(bf16[256,256]{1,0:T(8,128)(2,1)} %copy-done.4) | copy-start | bytes 393220
  141.3 18.0 %all-to-all-start.2 = ((bf16[16,2,8192]{2,1,0:T(2,128)(2,1)}), bf16[16,2,8192]{2,1,0:T(2,128)(2,1)S(1)}, u32[]{:S(2)}, u32[]{:S(2)}) async-start(bf16[16,2,8192]{2,1,0:T(2,128)(2,1)} %reshape.86), calls=%async_computation.2 | async-start | bytes 1048576 | tf_op jit(solution)/shard_map/all_to_all | solution.py:60
  144.9 16.3 %collective-permute-start.5 = (bf16[256,256]{1,0:T(8,128)(2,1)S(1)}, bf16[256,256]{1,0:T(8,128)(2,1)S(1)}, u32[]{:S(2)}, u32[]{:S(2)}) collective-permute-start(bf16[256,256]{1,0:T(8,128)(2,1)S(1)} %copy-done.5), channel_id=1, source_target_pairs={{1,0},{2,1},{3,2},{4,3},{5,4},{6,5},{7,6},{8,7},{9,8},{10,9},{11,1... | collective-permute-start | bytes 393224 | tf_op jit(solution)/shard_map/ppermute | solution.py:19
  146.2 15.6 %collective-permute-start.4 = (bf16[256,256]{1,0:T(8,128)(2,1)S(1)}, bf16[256,256]{1,0:T(8,128)(2,1)}, u32[]{:S(2)}, u32[]{:S(2)}) collective-permute-start(bf16[256,256]{1,0:T(8,128)(2,1)S(1)} %copy-done.5), channel_id=1, source_target_pairs={{0,1},{1,2},{2,3},{3,4},{4,5},{5,6},{6,7},{7,8},{8,9},{9,10},{10,1... | collective-permute-start | bytes 393224 | tf_op jit(solution)/shard_map/ppermute | solution.py:17
  161.2 0.6 copy-start.10
  191.9 5.7 %copy-start.7 = (f32[5]{0:T(128)S(1)}, f32[5]{0:T(128)}, u32[]{:S(2)}) copy-start(f32[5]{0:T(128)} %param.9) | copy-start | bytes 64
  194.0 18.0 %all-to-all-start.3 = ((bf16[16,2,8192]{2,1,0:T(2,128)(2,1)}), bf16[16,2,8192]{2,1,0:T(2,128)(2,1)S(1)}, u32[]{:S(2)}, u32[]{:S(2)}) async-start(bf16[16,2,8192]{2,1,0:T(2,128)(2,1)} %reshape.88), calls=%async_computation.3 | async-start | bytes 1048576 | tf_op jit(solution)/shard_map/all_to_all | solution.py:60
  198.3 15.6 %collective-permute-start.7 = (bf16[256,256]{1,0:T(8,128)(2,1)S(1)}, bf16[256,256]{1,0:T(8,128)(2,1)}, u32[]{:S(2)}, u32[]{:S(2)}) collective-permute-start(bf16[256,256]{1,0:T(8,128)(2,1)S(1)} %convert_bitcast_fusion), channel_id=1, source_target_pairs={{1,0},{2,1},{3,2},{4,3},{5,4},{6,5},{7,6},{8,7},{9,8},{10,9},{11,1... | collective-permute-start | bytes 393224 | tf_op jit(solution)/shard_map/ppermute | solution.py:19
  199.6 14.3 %collective-permute-start.6 = (bf16[256,256]{1,0:T(8,128)(2,1)S(1)}, bf16[256,256]{1,0:T(8,128)(2,1)}, u32[]{:S(2)}, u32[]{:S(2)}) collective-permute-start(bf16[256,256]{1,0:T(8,128)(2,1)S(1)} %convert_bitcast_fusion), channel_id=1, source_target_pairs={{0,1},{1,2},{2,3},{3,4},{4,5},{5,6},{6,7},{7,8},{8,9},{9,10},{10,1... | collective-permute-start | bytes 393224 | tf_op jit(solution)/shard_map/ppermute | solution.py:17
where the time goes:
time: 220 us; the launch traced here: 219 us
  blocking collectives  95.7 us (44%)
  waiting for transfers between devices  37.7 us (17%)
  starting transfers between devices  33.7 us (15%)
  matrix products  22.5 us (10%)
  local copies, waits for them, and re-layouts  21.1 us (10%)
  other arithmetic  8.06 us (4%)
    all_gather x4, blocking collectives, shards(): piece = lax.all_gather(flat_moments, 'blocks', axis=0, tiled=True)  95.7 us
    all_to_all x4, waiting for transfers between devices, shards(): lax.all_to_all(table.astype(jnp.bfloat16), 'blocks', split_axis=0, concat...  37.7 us
    unnamed x44, local copies, waits for them, and re-layouts  19.9 us
    all_to_all x4, starting transfers between devices, shards(): lax.all_to_all(table.astype(jnp.bfloat16), 'blocks', split_axis=0, concat...  14.4 us
    ppermute x4, starting transfers between devices, padded_2(): lax.ppermute(tail, axis, [(i, (i + 1) % count) for i in range(ends)])  14.1 us
    dot_general x4, matrix products, shards(): near = jnp.dot(near_tiles, padded, preferred_element_type=jnp.float32)  9.96 us
    ppermute x4, starting transfers between devices, padded_2(): lax.ppermute(head, axis, [((i + 1) % count, i) for i in range(ends)])  5.17 us
  transfers between devices with their start and end apart: 12, of which 4 were waited for; matrix products, arithmetic and copies ran while one was open for 4% of the time, Pallas kernels for 0%

commit v1 on v0

v1 whole, which is shorter than its diff:
```python
import functools

import jax
import jax.numpy as jnp
from jax import lax
from jax.experimental import pallas as pl
from jax.experimental.pallas import tpu as pltpu
from jax.sharding import PartitionSpec as P

ITERS = 4
MESH = pl.DeviceIdType.MESH


def steps(low, high, body):
    if high - low <= 8:
        for j in range(low, high):
            body(j)
    else:
        lax.fori_loop(low, high, lambda j, carry: (body(j), carry)[1], 0)


def chebyshev_kernel(
    count, coef, probes, col_basis, row_basis, near, local, out,
    moments, halo, current, partner_block, part_out, part_in, t_a, t_b,
    send_sem, recv_sem, halo_send, halo_recv, part_send, part_recv, block_sem,
):
    group = lax.axis_index("groups")
    me = lax.axis_index("blocks")
    chips = count // 2
    chip, core = me // 2, me % 2
    mate = me + 1 - 2 * core
    rank = row_basis.shape[1]

    def at(block):
        return (group, block)

    def plane(j):
        return 2 * lax.rem(chip + j, chips) + core

    barrier = pltpu.get_barrier_semaphore()

    def greet(block):
        pl.semaphore_signal(barrier, inc=1, device_id=at(block), device_id_type=MESH)

    steps(1, chips, lambda j: greet(plane(j)))
    greet(mate)
    far_side = me - 1 + 2 * core
    has_side = jnp.logical_and(far_side >= 0, far_side < count)

    @pl.when(has_side)
    def _():
        greet(far_side)

    pl.semaphore_wait(barrier, chips + jnp.where(has_side, 1, 0))

    has_left, has_right = me > 0, me < count - 1

    def remote(src, dst, sem_a, sem_b, block):
        return pltpu.make_async_remote_copy(
            src_ref=src, dst_ref=dst, send_sem=sem_a, recv_sem=sem_b,
            device_id=at(block), device_id_type=MESH,
        )

    def moment_copy(k, j):
        return remote(
            moments.at[k, chip], moments.at[k, chip], send_sem.at[k, j], recv_sem.at[k, j], plane(j)
        )

    def moment_arrival(k, j):
        source = lax.rem(chip + chips - j, chips)
        return remote(
            moments.at[k, source], moments.at[k, source], send_sem.at[k, j], recv_sem.at[k, j], plane(j)
        )

    def halo_copy(k, side):
        target = me + 1 if side == 0 else me - 1
        return remote(
            current.at[k], halo.at[k, side], halo_send.at[k, side], halo_recv.at[k, side], target
        )

    def part_copy(k):
        return remote(part_out.at[k], part_in.at[k], part_send.at[k], part_recv.at[k], mate)

    block_copy = remote(
        local.at[1 - core], partner_block, block_sem.at[0], block_sem.at[1], mate
    )

    @pl.when(jnp.logical_not(has_left))
    def _():
        for k in range(ITERS):
            halo[k, 0] = jnp.zeros(halo.shape[2:], halo.dtype)

    @pl.when(jnp.logical_not(has_right))
    def _():
        for k in range(ITERS):
            halo[k, 1] = jnp.zeros(halo.shape[2:], halo.dtype)

    rows = probes.shape[0]
    first = probes[...].astype(jnp.float32)
    t_a[...] = first
    out[...] = coef[0] * first
    for k in range(ITERS):
        now = t_a if k % 2 == 0 else t_b
        other = t_b if k % 2 == 0 else t_a
        cur = probes[...] if k == 0 else now[...].astype(jnp.bfloat16)
        current[k] = cur
        moments[k, chip] = lax.dot_general(
            col_basis[...], cur, (((0,), (0,)), ((), ())), preferred_element_type=jnp.float32
        ).astype(jnp.bfloat16)
        steps(1, chips, lambda j: moment_copy(k, j).start())

        @pl.when(has_right)
        def _():
            halo_copy(k, 0).start()

        @pl.when(has_left)
        def _():
            halo_copy(k, 1).start()

        if k == 0:
            block_copy.start()

        image = jnp.dot(
            near[:, rows : 2 * rows], current[k], preferred_element_type=jnp.float32
        )
        if k == 0:
            block_copy.wait()
        steps(1, chips, lambda j: moment_arrival(k, j).wait_recv())
        whole = moments[k].reshape(chips * rank, probes.shape[1])
        part_out[k] = jnp.dot(partner_block[...], whole, preferred_element_type=jnp.float32)
        part_copy(k).start()
        own = jnp.dot(local[core], whole, preferred_element_type=jnp.float32)

        @pl.when(has_left)
        def _():
            halo_copy(k, 0).wait_recv()

        image += jnp.dot(near[:, :rows], halo[k, 0], preferred_element_type=jnp.float32)

        @pl.when(has_right)
        def _():
            halo_copy(k, 1).wait_recv()

        image += jnp.dot(near[:, 2 * rows :], halo[k, 1], preferred_element_type=jnp.float32)
        part_copy(k).wait_recv()
        far = (own + part_in[k]).astype(jnp.bfloat16)
        image += jnp.dot(row_basis[...], far, preferred_element_type=jnp.float32)
        t_next = image if k == 0 else 2.0 * image - other[...]
        if k < ITERS - 1:
            other[...] = t_next
        out[...] += coef[k + 1] * t_next

    for k in range(ITERS):
        steps(1, chips, lambda j: moment_copy(k, j).wait_send())

        @pl.when(has_right)
        def _():
            halo_copy(k, 0).wait_send()

        @pl.when(has_left)
        def _():
            halo_copy(k, 1).wait_send()

        part_copy(k).wait_send()


def shards(probes, cheb_coef, col_basis, row_basis, near_tiles, coupling, far_rows, far_cols):
    leaf_count, rank = coupling.shape[0], coupling.shape[1]
    rows, width = probes.shape
    count = lax.axis_size("blocks")
    chips = count // 2
    cap = 2 * leaf_count // count
    ids = far_rows[:, 0]
    order = jnp.arange(leaf_count, dtype=jnp.int32)
    earlier = (ids[None, :] == ids[:, None]) & (order[None, :] < order[:, None])
    slot = ids * cap + jnp.sum(earlier.astype(jnp.int32), axis=1)
    place = (slot[None, :] == jnp.arange(count * cap, dtype=jnp.int32)[:, None]).astype(jnp.bfloat16)
    tag_width = -(-count // 128) * 128
    tags = (far_cols[:, None] == jnp.arange(tag_width, dtype=jnp.int32)[None, :]).astype(jnp.bfloat16)
    flat = jnp.concatenate([coupling.reshape(leaf_count, rank * rank), tags], axis=1)
    sent = jnp.dot(place, flat, preferred_element_type=jnp.float32).astype(jnp.bfloat16)
    got = lax.all_to_all(sent, "blocks", split_axis=0, concat_axis=0, tiled=True)
    mine = lax.dot_general(
        got[:, rank * rank : rank * rank + count], got[:, : rank * rank],
        (((0,), (0,)), ((), ())), preferred_element_type=jnp.float32,
    ).astype(jnp.bfloat16)
    local = mine.reshape(chips, 2, rank, rank).transpose(1, 2, 0, 3).reshape(2, rank, chips * rank)

    vmem = pl.BlockSpec(memory_space=pltpu.VMEM)
    dma = pltpu.SemaphoreType.DMA
    return pl.pallas_call(
        functools.partial(chebyshev_kernel, count),
        out_shape=jax.ShapeDtypeStruct((rows, width), jnp.float32),
        in_specs=[pl.BlockSpec(memory_space=pltpu.SMEM)] + [vmem] * 5,
        out_specs=vmem,
        scratch_shapes=[
            pltpu.VMEM((ITERS, chips, rank, width), jnp.bfloat16),
            pltpu.VMEM((ITERS, 2, rows, width), jnp.bfloat16),
            pltpu.VMEM((ITERS, rows, width), jnp.bfloat16),
            pltpu.VMEM((rank, chips * rank), jnp.bfloat16),
            pltpu.VMEM((ITERS, rank, width), jnp.float32),
            pltpu.VMEM((ITERS, rank, width), jnp.float32),
            pltpu.VMEM((rows, width), jnp.float32),
            pltpu.VMEM((rows, width), jnp.float32),
            dma((ITERS, chips)),
            dma((ITERS, chips)),
            dma((ITERS, 2)),
            dma((ITERS, 2)),
            dma((ITERS,)),
            dma((ITERS,)),
            dma((2,)),
        ],
        compiler_params=pltpu.CompilerParams(
            collective_id=0, has_side_effects=True, vmem_limit_bytes=32 * 1024 * 1024
        ),
    )(cheb_coef, probes, col_basis, row_basis, near_tiles, local)


def solution(mesh):
    return jax.shard_map(
        shards,
        mesh=mesh,
        in_specs=(
            P(("groups", "blocks"), None),
            P("groups"),
            P(("groups", "blocks"), None),
            P(("groups", "blocks"), None),
            P(("groups", "blocks"), None),
            P(("groups", "blocks"), None, None),
            P(("groups", "blocks"), None),
            P(("groups", "blocks")),
        ),
        out_specs=P(("groups", "blocks"), None),
        check_vma=False,
    )
```

time: 220 us -> 79.4 us (0.36)
  blocking collectives: 95.7 us -> 0 us
  Pallas kernels: 0 us -> 42.2 us
  starting transfers between devices: 33.7 us -> 7.51 us
  matrix products: 22.5 us -> 1.68 us
  local copies, waits for them, and re-layouts: 21.1 us -> 3.77 us
  waiting for transfers between devices: 37.7 us -> 23.2 us
  other arithmetic: 8.06 us -> 0.25 us
    all_gather x4 -> x0, blocking collectives: 95.7 us -> none  [shards(): piece = lax.all_gather(flat_moments, 'blocks', axis=0, tiled=True)]
    pallas_call x0 -> x1, Pallas kernels: none -> 42.2 us  [shards(): pl.pallas_call(functools.partial(chebyshev_kernel, count), out_shape=jax....]
    dot_general x28 -> x2, matrix products: 22.5 us -> 1.68 us  [the longest x1 1.42 us: shards(): jnp.dot(place, flat, preferred_element_type=jnp.float32)]
    ppermute x8 -> x0, starting transfers between devices: 19.3 us -> none  [the longest x4 14.1 us: padded_2(): lax.ppermute(tail, axis, [(i, (i + 1) % count) for i in range(ends)])]
    unnamed x44 -> x17, local copies, waits for them, and re-layouts: 19.9 us -> 1.04 us
    all_to_all x4 -> x1, waiting for transfers between devices: 37.7 us -> 23.2 us  [shards(): lax.all_to_all(sent, 'blocks', split_axis=0, concat_axis=0, tiled=True)]
    all_to_all x4 -> x1, starting transfers between devices: 14.4 us -> 7.51 us  [shards(): lax.all_to_all(sent, 'blocks', split_axis=0, concat_axis=0, tiled=True)]
    reduce_sum x4 -> x1, other arithmetic: 4.31 us -> 0.17 us  [shards(): slot = ids * cap + jnp.sum(earlier.astype(jnp.int32), axis=1)]
  transfers between devices with their start and end apart: 12 -> 1, of which waited for: 4 -> 1; matrix products, arithmetic and copies ran while one was open for 4% -> 0% of each run, Pallas kernels for 0% -> 0%
where the time goes in v1:
time: 79.4 us; the launch traced here: 78.7 us
  Pallas kernels  42.2 us (53%)
  waiting for transfers between devices  23.2 us (29%)
  starting transfers between devices  7.51 us (9%)
  local copies, waits for them, and re-layouts  3.77 us (5%)
  matrix products  1.68 us (2%)
    pallas_call x1, Pallas kernels, shards(): pl.pallas_call(functools.partial(chebyshev_kernel, count), out_shape=jax....  42.2 us
    all_to_all x1, waiting for transfers between devices, shards(): lax.all_to_all(sent, 'blocks', split_axis=0, concat_axis=0, tiled=True)  23.2 us
    all_to_all x1, starting transfers between devices, shards(): lax.all_to_all(sent, 'blocks', split_axis=0, concat_axis=0, tiled=True)  7.51 us
    reshape x1, local copies, waits for them, and re-layouts, shards(): coupling.reshape(leaf_count, rank * rank)  2.09 us
  transfers between devices with their start and end apart: 1, of which 1 were waited for; matrix products, arithmetic and copies ran while one was open for 0% of the time, Pallas kernels for 0%

profile of v1, /device:TPU:0, one launch (start us, length us, event | category | flops | bytes accessed | tf_op | source)
XLA Modules:
  0.0 78.7 jit_solution(1742927810634263848)
XLA Ops:
  0.0 0.0 copy-start.5
  0.0 0.0 copy-start.6
  0.0 2.1 %reshape.21 = bf16[64,4096]{1,0:T(8,128)(2,1)S(1)} reshape(bf16[64,64,64]{2,1,0:T(8,128)(2,1)} %param.13) | data formatting | bytes 1048576 | tf_op jit(solution)/shard_map/reshape | solution.py:180
  2.1 0.0 copy-done.5
  2.1 0.1 fusion.8
  2.2 0.0 copy-done.6
  2.2 0.2 convert_reduce_fusion
  2.4 1.4 %fusion = bf16[16,8,4224]{2,1,0:T(8,128)(2,1)} fusion(bf16[64,128]{1,0:T(8,128)(2,1)S(1)} %fusion.8, bf16[64,4096]{1,0:T(8,128)(2,1)S(1)} %reshape.21, s32[64]{0:T(128)S(1)} %multiply_add_fusion), kind=kOutput, calls=%fused_computation.1 | convolution fusion | flops 70836224 | bytes 1622272 | tf_op jit(solution)/shard_map/dot_general | solution.py:181
  3.8 0.0 copy-start.3
  3.8 0.0 copy-start.4
  3.8 7.5 %all-to-all-start = ((bf16[16,8,4224]{2,1,0:T(8,128)(2,1)}), bf16[16,8,4224]{2,1,0:T(8,128)(2,1)S(1)}, u32[]{:S(2)}, u32[]{:S(2)}) async-start(bf16[16,8,4224]{2,1,0:T(8,128)(2,1)} %fusion), calls=%async_computation | async-start | bytes 2162688 | tf_op jit(solution)/shard_map/all_to_all | solution.py:182
  11.3 0.0 copy-done.3
  11.3 0.1 copy.13.col_basis
  11.4 0.0 copy-done.4
  11.5 0.1 copy.14.row_basis
  11.6 23.2 %all-to-all-done = bf16[16,8,4224]{2,1,0:T(8,128)(2,1)S(1)} async-done(((bf16[16,8,4224]{2,1,0:T(8,128)(2,1)}), bf16[16,8,4224]{2,1,0:T(8,128)(2,1)S(1)}, u32[]{:S(2)}, u32[]{:S(2)}) %all-to-all-start) | async-done | bytes 1081376 | tf_op jit(solution)/shard_map/all_to_all | solution.py:182
  34.8 0.0 copy-start
  34.8 0.0 copy-start.1
  34.8 0.0 copy-start.2
  34.8 0.3 convolution_convert_fusion.1
  35.1 0.3 reshape.22
  35.4 0.2 copy.16
  35.5 0.2 reshape.23.local
  35.8 0.1 copy-done
  35.8 0.0 copy-done.1
  35.8 0.0 copy-done.2
  35.8 42.2 %shard_map.82 = f32[256,256]{1,0:T(8,128)S(1)} custom-call(f32[5]{0:T(128)S(1)} %copy-done.2, bf16[256,256]{1,0:T(8,128)(2,1)S(1)} %copy-done.1, bf16[256,64]{1,0:T(8,128)(2,1)S(1)} %copy.13.col_basis, bf16[256,64]{1,0:T(8,128)(2,1)S(1)} %copy.14.row_basis, bf16[256,768]{1,0:T(8,128)(2,1)S(1)} %copy-done, bf16[2,64,512]{2,1,0:T(8,128)(2,1)S(1)} %reshape.23.local), custom_call_target="tpu_custom_call" | custom-call | tf_op jit(solution)/shard_map/pallas_call | solution.py:191
  78.0 0.7 copy.18
  (1 shorter events, 0.0 us)
Async XLA Ops:
  0.0 2.1 %copy-start.5 = (s32[64]{0:T(128)S(1)}, s32[64]{0:T(128)}, u32[]{:S(2)}) copy-start(s32[64]{0:T(128)} %param.15) | copy-start | bytes 772
  0.0 2.2 %copy-start.6 = (s32[64,1]{0,1:T(1,128)S(1)}, s32[64,1]{0,1:T(1,128)}, u32[]{:S(2)}) copy-start(s32[64,1]{0,1:T(1,128)} %param.14) | copy-start | bytes 772
  3.8 7.5 %copy-start.3 = (bf16[256,64]{0,1:T(8,128)(2,1)S(1)}, bf16[256,64]{0,1:T(8,128)(2,1)}, u32[]{:S(2)}) copy-start(bf16[256,64]{0,1:T(8,128)(2,1)} %param.10) | copy-start | bytes 98308
  3.8 7.7 %copy-start.4 = (bf16[256,64]{0,1:T(8,128)(2,1)S(1)}, bf16[256,64]{0,1:T(8,128)(2,1)}, u32[]{:S(2)}) copy-start(bf16[256,64]{0,1:T(8,128)(2,1)} %param.11) | copy-start | bytes 98308
  3.8 31.0 %all-to-all-start = ((bf16[16,8,4224]{2,1,0:T(8,128)(2,1)}), bf16[16,8,4224]{2,1,0:T(8,128)(2,1)S(1)}, u32[]{:S(2)}, u32[]{:S(2)}) async-start(bf16[16,8,4224]{2,1,0:T(8,128)(2,1)} %fusion), calls=%async_computation | async-start | bytes 2162688 | tf_op jit(solution)/shard_map/all_to_all | solution.py:182
  34.8 1.0 %copy-start = (bf16[256,768]{1,0:T(8,128)(2,1)S(1)}, bf16[256,768]{1,0:T(8,128)(2,1)}, u32[]{:S(2)}) copy-start(bf16[256,768]{1,0:T(8,128)(2,1)} %near.1) | copy-start | bytes 1179652
  34.8 1.0 %copy-start.1 = (bf16[256,256]{1,0:T(8,128)(2,1)S(1)}, bf16[256,256]{1,0:T(8,128)(2,1)}, u32[]{:S(2)}) copy-start(bf16[256,256]{1,0:T(8,128)(2,1)} %probes.1) | copy-start | bytes 393220
  34.8 1.0 %copy-start.2 = (f32[5]{0:T(128)S(1)}, f32[5]{0:T(128)}, u32[]{:S(2)}) copy-start(f32[5]{0:T(128)} %coef.1) | copy-start | bytes 64

commit v2 on v1

v2 whole, which is shorter than its diff:
```python
import functools

import jax
import jax.numpy as jnp
from jax import lax
from jax.experimental import pallas as pl
from jax.experimental.pallas import tpu as pltpu
from jax.sharding import PartitionSpec as P

ITERS = 4
MESH = pl.DeviceIdType.MESH


def steps(low, high, body):
    if high - low <= 8:
        for j in range(low, high):
            body(j)
    else:
        lax.fori_loop(low, high, lambda j, carry: (body(j), carry)[1], 0)


def remote(src, dst, send, recv, target):
    return pltpu.make_async_remote_copy(
        src_ref=src, dst_ref=dst, send_sem=send, recv_sem=recv,
        device_id=target, device_id_type=MESH,
    )


def position():
    group, me = lax.axis_index("groups"), lax.axis_index("blocks")
    return lambda block: (group, block), me


def greet(target):
    pl.semaphore_signal(
        pltpu.get_barrier_semaphore(), inc=1, device_id=target, device_id_type=MESH
    )


def moments_of(basis, cur):
    return lax.dot_general(
        basis, cur, (((0,), (0,)), ((), ())), preferred_element_type=jnp.float32
    ).astype(jnp.bfloat16)


def start_kernel(
    count, probes, col_basis, near, slots, got, moments, near_out,
    halo, send_sem, recv_sem, slot_send, slot_recv, halo_send, halo_recv,
):
    at, me = position()
    chips = count // 2
    pairs = chips // 2
    chip, core = me // 2, me % 2
    pair, side = chip // 2, chip % 2
    rows = probes.shape[0]

    def plane(j):
        return at(2 * lax.rem(chip + j, chips) + core)

    def line(j):
        return at(4 * lax.rem(pair + j, pairs) + 2 * side + core)

    has_left, has_right = me > 0, me < count - 1
    steps(1, chips, lambda j: greet(plane(j)))
    greet(at(me + 1 - 2 * core))
    outer = me - 1 + 2 * core
    has_outer = jnp.logical_and(outer >= 0, outer < count)

    @pl.when(has_outer)
    def _():
        greet(at(outer))

    moments[pair] = moments_of(col_basis[...], probes[...])

    @pl.when(jnp.logical_not(has_left))
    def _():
        halo[0] = jnp.zeros(probes.shape, halo.dtype)

    @pl.when(jnp.logical_not(has_right))
    def _():
        halo[1] = jnp.zeros(probes.shape, halo.dtype)

    pl.semaphore_wait(pltpu.get_barrier_semaphore(), chips + jnp.where(has_outer, 1, 0))

    def slot_copy(j):
        return remote(
            slots.at[lax.rem(chip + j, chips)], got.at[chip], slot_send.at[j], slot_recv.at[j], plane(j)
        )

    def slot_arrival(j):
        source = lax.rem(chip + chips - j, chips)
        return remote(slots.at[source], got.at[source], slot_send.at[j], slot_recv.at[j], plane(j))

    def moment_copy(j):
        return remote(moments.at[pair], moments.at[pair], send_sem.at[j], recv_sem.at[j], line(j))

    def moment_arrival(j):
        source = lax.rem(pair + pairs - j, pairs)
        return remote(moments.at[source], moments.at[source], send_sem.at[j], recv_sem.at[j], line(j))

    def halo_copy(way):
        target = me + 1 if way == 0 else me - 1
        return remote(probes, halo.at[way], halo_send.at[way], halo_recv.at[way], at(target))

    steps(1, chips, lambda j: slot_copy(j).start())

    @pl.when(has_right)
    def _():
        halo_copy(0).start()

    @pl.when(has_left)
    def _():
        halo_copy(1).start()

    steps(1, pairs, lambda j: moment_copy(j).start())
    got[chip] = slots[chip]
    near_out[...] = jnp.dot(
        near[:, rows : 2 * rows], probes[...], preferred_element_type=jnp.float32
    )

    @pl.when(has_left)
    def _():
        halo_copy(0).wait_recv()

    near_out[...] += jnp.dot(near[:, :rows], halo[0], preferred_element_type=jnp.float32)

    @pl.when(has_right)
    def _():
        halo_copy(1).wait_recv()

    near_out[...] += jnp.dot(near[:, 2 * rows :], halo[1], preferred_element_type=jnp.float32)
    steps(1, pairs, lambda j: moment_arrival(j).wait_recv())
    steps(1, chips, lambda j: slot_arrival(j).wait_recv())
    steps(1, pairs, lambda j: moment_copy(j).wait_send())
    steps(1, chips, lambda j: slot_copy(j).wait_send())

    @pl.when(has_right)
    def _():
        halo_copy(0).wait_send()

    @pl.when(has_left)
    def _():
        halo_copy(1).wait_send()


def chebyshev_kernel(
    count, coef, probes, col_basis, row_basis, near, pieces, moments_0, near_0, out,
    moments, halo, current, blocks, local, part_out, part_in, t_a, t_b,
    send_sem, recv_sem, halo_send, halo_recv, part_send, part_recv, block_send, block_recv,
):
    at, me = position()
    pairs = count // 4
    pair, quarter = me // 4, me % 4
    rows, width = probes.shape
    rank = row_basis.shape[1]

    def line(j):
        return at(4 * lax.rem(pair + j, pairs) + quarter)

    def beside(j):
        return lax.rem(quarter + j, 4)

    def room(j):
        return at(4 * pair + beside(j))

    has_left, has_right = me > 0, me < count - 1
    steps(1, pairs, lambda j: greet(line(j)))
    steps(1, 4, lambda j: greet(room(j)))
    outer_left = jnp.logical_and(quarter == 0, has_left)
    outer_right = jnp.logical_and(quarter == 3, has_right)

    @pl.when(outer_left)
    def _():
        greet(at(me - 1))

    @pl.when(outer_right)
    def _():
        greet(at(me + 1))

    @pl.when(jnp.logical_not(has_left))
    def _():
        for k in range(1, ITERS):
            halo[k, 0] = jnp.zeros(probes.shape, halo.dtype)

    @pl.when(jnp.logical_not(has_right))
    def _():
        for k in range(1, ITERS):
            halo[k, 1] = jnp.zeros(probes.shape, halo.dtype)

    extra = jnp.where(jnp.logical_or(outer_left, outer_right), 1, 0)
    pl.semaphore_wait(pltpu.get_barrier_semaphore(), pairs + 2 + extra)

    def moment_copy(k, j):
        return remote(
            moments.at[k, pair], moments.at[k, pair], send_sem.at[k, j], recv_sem.at[k, j], line(j)
        )

    def moment_arrival(k, j):
        source = lax.rem(pair + pairs - j, pairs)
        return remote(
            moments.at[k, source], moments.at[k, source], send_sem.at[k, j], recv_sem.at[k, j], line(j)
        )

    def halo_copy(k, way):
        target = me + 1 if way == 0 else me - 1
        return remote(
            current.at[k], halo.at[k, way], halo_send.at[k, way], halo_recv.at[k, way], at(target)
        )

    def part_copy(k, j):
        return remote(
            part_out.at[k, beside(j)], part_in.at[k, quarter], part_send.at[k, j], part_recv.at[k, j], room(j)
        )

    def part_arrival(k, j):
        source = beside(4 - j)
        return remote(
            part_out.at[k, source], part_in.at[k, source], part_send.at[k, j], part_recv.at[k, j], room(j)
        )

    def block_copy(j):
        return remote(
            pieces.at[beside(j)], blocks.at[quarter], block_send.at[j], block_recv.at[j], room(j)
        )

    def block_arrival(j):
        source = beside(4 - j)
        return remote(pieces.at[source], blocks.at[source], block_send.at[j], block_recv.at[j], room(j))

    steps(1, 4, lambda j: block_copy(j).start())
    blocks[quarter] = pieces[quarter]
    first = probes[...].astype(jnp.float32)
    t_a[...] = first
    out[...] = coef[0] * first
    steps(1, 4, lambda j: block_arrival(j).wait_recv())
    half = 2 * rank
    for s in range(2):
        local[s * half : (s + 1) * half, :] = (
            blocks[2 * s].astype(jnp.float32) + blocks[2 * s + 1].astype(jnp.float32)
        ).astype(jnp.bfloat16)

    for k in range(ITERS):
        now = t_a if k % 2 == 0 else t_b
        other = t_b if k % 2 == 0 else t_a
        if k > 0:
            cur = now[...].astype(jnp.bfloat16)
            moments[k, pair] = moments_of(col_basis[...], cur)
            steps(1, pairs, lambda j: moment_copy(k, j).start())
            current[k] = cur

            @pl.when(has_right)
            def _():
                halo_copy(k, 0).start()

            @pl.when(has_left)
            def _():
                halo_copy(k, 1).start()

            near_out = jnp.dot(
                near[:, rows : 2 * rows], current[k], preferred_element_type=jnp.float32
            )
            steps(1, pairs, lambda j: moment_arrival(k, j).wait_recv())
            held = moments[k]
        else:
            held = moments_0[...]
            near_out = near_0[...]
        parts = jnp.dot(
            local[...], held.reshape(pairs * rank, width), preferred_element_type=jnp.float32
        )
        part_out[k] = parts.astype(jnp.bfloat16).reshape(4, rank, width)
        steps(1, 4, lambda j: part_copy(k, j).start())
        part_in[k, quarter] = part_out[k, quarter]
        if k > 0:

            @pl.when(has_left)
            def _():
                halo_copy(k, 0).wait_recv()

            near_out += jnp.dot(near[:, :rows], halo[k, 0], preferred_element_type=jnp.float32)

            @pl.when(has_right)
            def _():
                halo_copy(k, 1).wait_recv()

            near_out += jnp.dot(near[:, 2 * rows :], halo[k, 1], preferred_element_type=jnp.float32)
        steps(1, 4, lambda j: part_arrival(k, j).wait_recv())
        far = jnp.sum(part_in[k].astype(jnp.float32), axis=0).astype(jnp.bfloat16)
        image = near_out + jnp.dot(row_basis[...], far, preferred_element_type=jnp.float32)
        t_next = image if k == 0 else 2.0 * image - other[...]
        if k < ITERS - 1:
            other[...] = t_next
        out[...] += coef[k + 1] * t_next

    steps(1, 4, lambda j: block_copy(j).wait_send())
    for k in range(ITERS):
        if k > 0:
            steps(1, pairs, lambda j: moment_copy(k, j).wait_send())

            @pl.when(has_right)
            def _():
                halo_copy(k, 0).wait_send()

            @pl.when(has_left)
            def _():
                halo_copy(k, 1).wait_send()

        steps(1, 4, lambda j: part_copy(k, j).wait_send())


def shards(probes, cheb_coef, col_basis, row_basis, near_tiles, coupling, far_rows, far_cols):
    leaf_count, rank = coupling.shape[0], coupling.shape[1]
    rows, width = probes.shape
    count = lax.axis_size("blocks")
    chips, pairs = count // 2, count // 4
    cap = 2 * leaf_count // count
    depth = -(-2 * cap // 16) * 16
    ids = far_rows[:, 0]
    order = jnp.arange(leaf_count, dtype=jnp.int32)
    earlier = (ids[None, :] == ids[:, None]) & (order[None, :] < order[:, None])
    nth = jnp.sum(earlier.astype(jnp.int32), axis=1)
    slot = (ids // 2) * depth + (ids % 2) * cap + nth
    place = (slot[None, :] == jnp.arange(chips * depth, dtype=jnp.int32)[:, None]).astype(jnp.bfloat16)
    tag_width = -(-2 * count // 128) * 128
    tag = (ids % 2) * count + far_cols
    tags = (tag[:, None] == jnp.arange(tag_width, dtype=jnp.int32)[None, :]).astype(jnp.bfloat16)
    flat = jnp.concatenate([coupling.reshape(leaf_count, rank * rank), tags], axis=1)
    sent = jnp.dot(place, flat, preferred_element_type=jnp.float32).astype(jnp.bfloat16)
    sent = sent.reshape(chips, depth, flat.shape[1])

    vmem = pl.BlockSpec(memory_space=pltpu.VMEM)
    dma = pltpu.SemaphoreType.DMA
    grant = 48 * 1024 * 1024
    got, moments_0, near_0 = pl.pallas_call(
        functools.partial(start_kernel, count),
        out_shape=[
            jax.ShapeDtypeStruct(sent.shape, jnp.bfloat16),
            jax.ShapeDtypeStruct((pairs, rank, width), jnp.bfloat16),
            jax.ShapeDtypeStruct((rows, width), jnp.float32),
        ],
        in_specs=[vmem] * 4,
        out_specs=[vmem] * 3,
        scratch_shapes=[
            pltpu.VMEM((2, rows, width), jnp.bfloat16),
            dma((pairs,)), dma((pairs,)), dma((chips,)), dma((chips,)), dma((2,)), dma((2,)),
        ],
        compiler_params=pltpu.CompilerParams(
            collective_id=0, has_side_effects=True, vmem_limit_bytes=grant
        ),
    )(probes, col_basis, near_tiles, sent)

    got = got.reshape(chips * depth, flat.shape[1])
    mine = lax.dot_general(
        got[:, rank * rank : rank * rank + 2 * count], got[:, : rank * rank],
        (((0,), (0,)), ((), ())), preferred_element_type=jnp.float32,
    ).astype(jnp.bfloat16)
    pieces = mine.reshape(2, pairs, 4, rank, rank).transpose(2, 0, 3, 1, 4)
    pieces = pieces.reshape(4, 2 * rank, pairs * rank)

    return pl.pallas_call(
        functools.partial(chebyshev_kernel, count),
        out_shape=jax.ShapeDtypeStruct((rows, width), jnp.float32),
        in_specs=[pl.BlockSpec(memory_space=pltpu.SMEM)] + [vmem] * 7,
        out_specs=vmem,
        scratch_shapes=[
            pltpu.VMEM((ITERS, pairs, rank, width), jnp.bfloat16),
            pltpu.VMEM((ITERS, 2, rows, width), jnp.bfloat16),
            pltpu.VMEM((ITERS, rows, width), jnp.bfloat16),
            pltpu.VMEM((4, 2 * rank, pairs * rank), jnp.bfloat16),
            pltpu.VMEM((4 * rank, pairs * rank), jnp.bfloat16),
            pltpu.VMEM((ITERS, 4, rank, width), jnp.bfloat16),
            pltpu.VMEM((ITERS, 4, rank, width), jnp.bfloat16),
            pltpu.VMEM((rows, width), jnp.float32),
            pltpu.VMEM((rows, width), jnp.float32),
            dma((ITERS, pairs)), dma((ITERS, pairs)), dma((ITERS, 2)), dma((ITERS, 2)),
            dma((ITERS, 4)), dma((ITERS, 4)), dma((4,)), dma((4,)),
        ],
        compiler_params=pltpu.CompilerParams(
            collective_id=1, has_side_effects=True, vmem_limit_bytes=grant
        ),
    )(cheb_coef, probes, col_basis, row_basis, near_tiles, pieces, moments_0, near_0)


def solution(mesh):
    return jax.shard_map(
        shards,
        mesh=mesh,
        in_specs=(
            P(("groups", "blocks"), None),
            P("groups"),
            P(("groups", "blocks"), None),
            P(("groups", "blocks"), None),
            P(("groups", "blocks"), None),
            P(("groups", "blocks"), None, None),
            P(("groups", "blocks"), None),
            P(("groups", "blocks")),
        ),
        out_specs=P(("groups", "blocks"), None),
        check_vma=False,
    )
```

time: 79.4 us -> 77.7 us (0.979)
  Pallas kernels: 42.2 us -> 70.2 us
  waiting for transfers between devices: 23.2 us -> 0 us
  starting transfers between devices: 7.51 us -> 0 us
  other arithmetic: 0.25 us -> 1.67 us
  local copies, waits for them, and re-layouts: 3.77 us -> 4.77 us
  matrix products: 1.68 us -> 0.72 us
    pallas_call x0 -> x1, Pallas kernels: none -> 34.4 us  [shards(): pl.pallas_call(functools.partial(start_kernel, count), out_shape=[jax.Sha...]
    all_to_all x1 -> x0, waiting for transfers between devices: 23.2 us -> none  [shards(): lax.all_to_all(sent, 'blocks', split_axis=0, concat_axis=0, tiled=True)]
    all_to_all x1 -> x0, starting transfers between devices: 7.51 us -> none  [shards(): lax.all_to_all(sent, 'blocks', split_axis=0, concat_axis=0, tiled=True)]
    pallas_call x1, Pallas kernels: 42.2 us -> 35.8 us  [shards(): pl.pallas_call(functools.partial(chebyshev_kernel, count), out_shape=jax....]
    dot_general x1, matrix products: 1.42 us -> 0.42 us  [shards(): jnp.dot(place, flat, preferred_element_type=jnp.float32)]
  transfers between devices with their start and end apart: 1 -> 0, of which waited for: 1 -> 0; matrix products, arithmetic and copies ran while one was open for 0% -> 0% of each run, Pallas kernels for 0% -> 0%
where the time goes in v2:
time: 77.7 us; the launch traced here: 77.5 us
  Pallas kernels  70.2 us (90%)
  local copies, waits for them, and re-layouts  4.77 us (6%)
  other arithmetic  1.67 us (2%)
    pallas_call x1, Pallas kernels, shards(): pl.pallas_call(functools.partial(chebyshev_kernel, count), out_shape=jax....  35.8 us
    pallas_call x1, Pallas kernels, shards(): pl.pallas_call(functools.partial(start_kernel, count), out_shape=[jax.Sha...  34.4 us
    reshape x1, local copies, waits for them, and re-layouts, shards(): coupling.reshape(leaf_count, rank * rank)  2.07 us

profile of v2, /device:TPU:0, one launch (start us, length us, event | category | flops | bytes accessed | tf_op | source)
XLA Modules:
  0.0 77.5 jit_solution(16809793455588961252)
XLA Ops:
  0.0 0.9 %convert_reduce_fusion = s32[64]{0:T(128)S(1)} fusion(s32[64]{0:T(128)} %bitcast.15), kind=kLoop, calls=%fused_computation.11 | loop fusion | flops 20416 | bytes 512 | tf_op jit(solution)/shard_map/reduce_sum | solution.py:320
  0.9 0.7 add_add_fusion
  1.6 0.1 fusion.7
  1.7 2.1 %reshape.71 = bf16[64,4096]{1,0:T(8,128)(2,1)S(1)} reshape(bf16[64,64,64]{2,1,0:T(8,128)(2,1)} %param.13) | data formatting | bytes 1048576 | tf_op jit(solution)/shard_map/reshape | solution.py:326
  3.8 0.0 copy-start.3
  3.8 0.0 copy-start
  3.8 0.0 copy-start.1
  3.8 0.4 convolution_convert_fusion
  4.2 0.3 copy-done.3
  4.5 0.1 copy.15.col_basis
  4.6 0.1 copy-done
  4.8 0.0 copy-done.1
  4.8 34.4 %shard_map.82 = (bf16[8,16,4224]{2,1,0:T(8,128)(2,1)S(1)}, bf16[4,64,256]{2,1,0:T(8,128)(2,1)S(1)}, f32[256,256]{1,0:T(8,128)S(1)}) custom-call(bf16[256,256]{1,0:T(8,128)(2,1)S(1)} %copy-done.1, bf16[256,64]{1,0:T(8,128)(2,1)S(1)} %copy.15.col_basis, bf16[256,768]{1,0:T(8,128)(2,1)S(1)} %copy-done, bf16[8,16,4224]{2,1,0:T(8,128)(2,1)S(1)} %bitcast.12), custom_call_target="tpu_custom_call" | custom-call | tf_op jit(solution)/shard_map/pallas_call | solution.py:333
  39.2 0.3 convolution_convert_fusion.1
  39.5 0.5 reshape.74
  40.1 0.0 copy-start.4
  40.1 0.0 copy-start.2
  40.1 0.4 copy.18
  40.5 0.3 reshape.75.pieces
  40.9 0.0 copy-done.4
  40.9 0.1 copy.16.row_basis
  41.0 0.0 copy-done.2
  41.0 35.8 %shard_map.83 = f32[256,256]{1,0:T(8,128)S(1)} custom-call(f32[5]{0:T(128)S(1)} %copy-done.2, bf16[256,256]{1,0:T(8,128)(2,1)S(1)} %copy-done.1, bf16[256,64]{1,0:T(8,128)(2,1)S(1)} %copy.15.col_basis, bf16[256,64]{1,0:T(8,128)(2,1)S(1)} %copy.16.row_basis, bf16[256,768]{1,0:T(8,128)(2,1)S(1)} %copy-done, bf16[4,128,256]{2,1,0:T(8,128)(2,1)S(1)} %reshape.75.pieces, ...), custom_call_target="tpu_custom_call" | custom-call | tf_op jit(solution)/shard_map/pallas_call | solution.py:359
  76.8 0.7 copy.20
Async XLA Ops:
  3.8 0.8 copy-start.3
  3.8 1.0 %copy-start = (bf16[256,768]{1,0:T(8,128)(2,1)S(1)}, bf16[256,768]{1,0:T(8,128)(2,1)}, u32[]{:S(2)}) copy-start(bf16[256,768]{1,0:T(8,128)(2,1)} %near.3) | copy-start | bytes 1179652
  3.8 1.0 %copy-start.1 = (bf16[256,256]{1,0:T(8,128)(2,1)S(1)}, bf16[256,256]{1,0:T(8,128)(2,1)}, u32[]{:S(2)}) copy-start(bf16[256,256]{1,0:T(8,128)(2,1)} %probes.3) | copy-start | bytes 393220
  40.1 0.8 %copy-start.4 = (bf16[256,64]{0,1:T(8,128)(2,1)S(1)}, bf16[256,64]{0,1:T(8,128)(2,1)}, u32[]{:S(2)}) copy-start(bf16[256,64]{0,1:T(8,128)(2,1)} %param.11) | copy-start | bytes 98308
  40.1 0.9 %copy-start.2 = (f32[5]{0:T(128)S(1)}, f32[5]{0:T(128)}, u32[]{:S(2)}) copy-start(f32[5]{0:T(128)} %coef.1) | copy-start | bytes 64

commit v3 on v2

v3 whole, which is shorter than its diff:
```python
import functools

import jax
import jax.numpy as jnp
from jax import lax
from jax.experimental import pallas as pl
from jax.experimental.pallas import tpu as pltpu
from jax.sharding import PartitionSpec as P

ITERS = 4
LANES = 128
MESH = pl.DeviceIdType.MESH


def steps(low, high, body):
    if high - low <= 8:
        for j in range(low, high):
            body(j)
    else:
        lax.fori_loop(low, high, lambda j, carry: (body(j), carry)[1], 0)


def remote(src, dst, send, recv, target):
    return pltpu.make_async_remote_copy(
        src_ref=src, dst_ref=dst, send_sem=send, recv_sem=recv,
        device_id=target, device_id_type=MESH,
    )


def position():
    group, me = lax.axis_index("groups"), lax.axis_index("blocks")
    return lambda block: (group, block), me


def greet(target):
    pl.semaphore_signal(
        pltpu.get_barrier_semaphore(), inc=1, device_id=target, device_id_type=MESH
    )


def start_kernel(
    count, probes, col_basis, near, slots, got, moments, near_out, basis_t,
    halo, send_sem, recv_sem, slot_send, slot_recv, halo_send, halo_recv,
    mate_sem,
):
    at, me = position()
    chips = count // 2
    pairs = chips // 2
    chip, core = me // 2, me % 2
    pair, side = chip // 2, chip % 2
    rows = probes.shape[0]

    def plane(j):
        return at(2 * lax.rem(chip + j, chips) + core)

    mate = at(me + 1 - 2 * core)
    has_left, has_right = me > 0, me < count - 1
    steps(1, chips, lambda j: greet(plane(j)))
    greet(mate)
    outer = me - 1 + 2 * core
    has_outer = jnp.logical_and(outer >= 0, outer < count)

    @pl.when(has_outer)
    def _():
        greet(at(outer))

    basis_t[...] = col_basis[...].T
    moments[core, side, pair] = jnp.dot(
        basis_t[...], probes[...], preferred_element_type=jnp.float32
    ).astype(jnp.bfloat16)

    @pl.when(jnp.logical_not(has_left))
    def _():
        halo[0] = jnp.zeros(probes.shape, halo.dtype)

    @pl.when(jnp.logical_not(has_right))
    def _():
        halo[1] = jnp.zeros(probes.shape, halo.dtype)

    pl.semaphore_wait(pltpu.get_barrier_semaphore(), chips + jnp.where(has_outer, 1, 0))

    def slot_copy(j):
        return remote(
            slots.at[lax.rem(chip + j, chips)], got.at[chip], slot_send.at[j], slot_recv.at[j], plane(j)
        )

    def slot_arrival(j):
        source = lax.rem(chip + chips - j, chips)
        return remote(slots.at[source], got.at[source], slot_send.at[j], slot_recv.at[j], plane(j))

    def moment_copy(j):
        own = moments.at[core, side, pair]
        return remote(own, own, send_sem.at[j], recv_sem.at[j], plane(j))

    def moment_arrival(j):
        source = lax.rem(chip + chips - j, chips)
        held = moments.at[core, lax.rem(source, 2), source // 2]
        return remote(held, held, send_sem.at[j], recv_sem.at[j], plane(j))

    mate_copy = remote(moments.at[core], moments.at[core], mate_sem.at[0], mate_sem.at[1], mate)
    mate_arrival = remote(
        moments.at[1 - core], moments.at[1 - core], mate_sem.at[0], mate_sem.at[1], mate
    )

    def halo_copy(way):
        target = me + 1 if way == 0 else me - 1
        return remote(probes, halo.at[way], halo_send.at[way], halo_recv.at[way], at(target))

    steps(1, chips, lambda j: moment_copy(j).start())
    steps(1, chips, lambda j: slot_copy(j).start())

    @pl.when(has_right)
    def _():
        halo_copy(0).start()

    @pl.when(has_left)
    def _():
        halo_copy(1).start()

    got[chip] = slots[chip]
    steps(1, chips, lambda j: moment_arrival(j).wait_recv())
    mate_copy.start()
    near_out[...] = jnp.dot(
        near[:, rows : 2 * rows], probes[...], preferred_element_type=jnp.float32
    )

    @pl.when(has_left)
    def _():
        halo_copy(0).wait_recv()

    near_out[...] += jnp.dot(near[:, :rows], halo[0], preferred_element_type=jnp.float32)

    @pl.when(has_right)
    def _():
        halo_copy(1).wait_recv()

    near_out[...] += jnp.dot(near[:, 2 * rows :], halo[1], preferred_element_type=jnp.float32)
    mate_arrival.wait_recv()
    steps(1, chips, lambda j: slot_arrival(j).wait_recv())
    mate_copy.wait_send()
    steps(1, chips, lambda j: moment_copy(j).wait_send())
    steps(1, chips, lambda j: slot_copy(j).wait_send())

    @pl.when(has_right)
    def _():
        halo_copy(0).wait_send()

    @pl.when(has_left)
    def _():
        halo_copy(1).wait_send()


def chebyshev_kernel(
    count, coef, probes, basis_t, row_basis, near, pieces, moments_0, near_0, out,
    moments, halo, current, blocks, local, part_out, part_in, t_a, t_b, near_sum,
    send_sem, recv_sem, halo_send, halo_recv, part_send, part_recv, block_send, block_recv,
):
    at, me = position()
    pairs = count // 4
    pair, quarter = me // 4, me % 4
    rows, width = probes.shape
    rank = row_basis.shape[1]
    lanes = current.shape[2]
    streams = width // lanes

    def line(j):
        return at(4 * lax.rem(pair + j, pairs) + quarter)

    def beside(j):
        return lax.rem(quarter + j, 4)

    def room(j):
        return at(4 * pair + beside(j))

    has_left, has_right = me > 0, me < count - 1
    steps(1, pairs, lambda j: greet(line(j)))
    steps(1, 4, lambda j: greet(room(j)))
    outer_left = jnp.logical_and(quarter == 0, has_left)
    outer_right = jnp.logical_and(quarter == 3, has_right)

    @pl.when(outer_left)
    def _():
        greet(at(me - 1))

    @pl.when(outer_right)
    def _():
        greet(at(me + 1))

    @pl.when(jnp.logical_not(has_left))
    def _():
        for q in range(streams, ITERS * streams):
            halo[q, 0] = jnp.zeros(halo.shape[2:], halo.dtype)

    @pl.when(jnp.logical_not(has_right))
    def _():
        for q in range(streams, ITERS * streams):
            halo[q, 1] = jnp.zeros(halo.shape[2:], halo.dtype)

    extra = jnp.where(jnp.logical_or(outer_left, outer_right), 1, 0)
    pl.semaphore_wait(pltpu.get_barrier_semaphore(), pairs + 2 + extra)

    def moment_copy(q, j):
        return remote(
            moments.at[q, pair], moments.at[q, pair], send_sem.at[q, j], recv_sem.at[q, j], line(j)
        )

    def moment_arrival(q, j):
        source = lax.rem(pair + pairs - j, pairs)
        return remote(
            moments.at[q, source], moments.at[q, source], send_sem.at[q, j], recv_sem.at[q, j], line(j)
        )

    def halo_copy(q, way):
        target = me + 1 if way == 0 else me - 1
        return remote(
            current.at[q], halo.at[q, way], halo_send.at[q, way], halo_recv.at[q, way], at(target)
        )

    def part_copy(q, j):
        return remote(
            part_out.at[q, beside(j)], part_in.at[q, quarter], part_send.at[q, j], part_recv.at[q, j], room(j)
        )

    def part_arrival(q, j):
        source = beside(4 - j)
        return remote(
            part_out.at[q, source], part_in.at[q, source], part_send.at[q, j], part_recv.at[q, j], room(j)
        )

    def block_copy(j):
        return remote(
            pieces.at[beside(j)], blocks.at[quarter], block_send.at[j], block_recv.at[j], room(j)
        )

    def block_arrival(j):
        source = beside(4 - j)
        return remote(pieces.at[source], blocks.at[source], block_send.at[j], block_recv.at[j], room(j))

    steps(1, 4, lambda j: block_copy(j).start())
    blocks[quarter] = pieces[quarter]
    first = probes[...].astype(jnp.float32)
    t_a[...] = first
    out[...] = coef[0] * first
    half = 2 * rank
    core = lax.rem(quarter, 2)
    mix = jnp.dot(
        basis_t[...], row_basis[...], preferred_element_type=jnp.float32
    ).astype(jnp.bfloat16)

    def gather_blocks():
        steps(1, 4, lambda j: block_arrival(j).wait_recv())
        for s in range(2):
            local[s * half : (s + 1) * half, :] = (
                blocks[2 * s].astype(jnp.float32) + blocks[2 * s + 1].astype(jnp.float32)
            ).astype(jnp.bfloat16)

    def mate_part(q):
        return remote(
            part_out.at[q, 1 - core], part_in.at[q, core], part_send.at[q, 0], part_recv.at[q, 0],
            at(me + 1 - 2 * core),
        )

    def mate_part_arrival(q):
        return remote(
            part_out.at[q, 1 - core], part_in.at[q, 1 - core], part_send.at[q, 0], part_recv.at[q, 0],
            at(me + 1 - 2 * core),
        )

    def columns(h):
        return slice(h * lanes, (h + 1) * lanes)

    def buffers(k):
        return (t_a, t_b) if k % 2 == 0 else (t_b, t_a)

    def part_stage(k, h):
        q = k * streams + h
        if k == 0:
            parts = jnp.zeros((half, lanes), jnp.float32)
            for c in range(4):
                held = moments_0[c % 2, c // 2, :, :, columns(h)]
                parts += jnp.dot(
                    pieces[c], held.reshape(pairs * rank, lanes), preferred_element_type=jnp.float32
                )
            part_out[q, 0:2] = parts.astype(jnp.bfloat16).reshape(2, rank, lanes)
            mate_part(q).start()
            part_in[q, core] = part_out[q, core]
        else:
            steps(1, pairs, lambda j: moment_arrival(q, j).wait_recv())
            parts = jnp.dot(
                local[...], moments[q].reshape(pairs * rank, lanes), preferred_element_type=jnp.float32
            )
            part_out[q] = parts.astype(jnp.bfloat16).reshape(4, rank, lanes)
            steps(1, 4, lambda j: part_copy(q, j).start())
            part_in[q, quarter] = part_out[q, quarter]
            near_sum[:, columns(h)] = jnp.dot(
                near[:, rows : 2 * rows], current[q], preferred_element_type=jnp.float32
            )

    def finish_stage(k, h):
        q = k * streams + h
        other = buffers(k)[1]
        if k > 0:
            near_out = near_sum[:, columns(h)]

            @pl.when(has_left)
            def _():
                halo_copy(q, 0).wait_recv()

            near_out += jnp.dot(near[:, :rows], halo[q, 0], preferred_element_type=jnp.float32)

            @pl.when(has_right)
            def _():
                halo_copy(q, 1).wait_recv()

            near_out += jnp.dot(near[:, 2 * rows :], halo[q, 1], preferred_element_type=jnp.float32)
            near_out = 2.0 * near_out - other[:, columns(h)]
        else:
            near_out = near_0[:, columns(h)]
        last = k == ITERS - 1
        if not last:
            later = q + streams
            base = jnp.dot(
                basis_t[...], near_out.astype(jnp.bfloat16), preferred_element_type=jnp.float32
            )
        if k == 0:
            mate_part_arrival(q).wait_recv()
            far = jnp.sum(part_in[q, 0:2].astype(jnp.float32), axis=0).astype(jnp.bfloat16)
            weight = 1.0
        else:
            steps(1, 4, lambda j: part_arrival(q, j).wait_recv())
            far = jnp.sum(part_in[q].astype(jnp.float32), axis=0).astype(jnp.bfloat16)
            weight = 2.0
        if not last:
            base += weight * jnp.dot(mix, far, preferred_element_type=jnp.float32)
            moments[later, pair] = base.astype(jnp.bfloat16)
            steps(1, pairs, lambda j: moment_copy(later, j).start())
        t_next = near_out + weight * jnp.dot(
            row_basis[...], far, preferred_element_type=jnp.float32
        )
        if not last:
            current[later] = t_next.astype(jnp.bfloat16)

            @pl.when(has_right)
            def _():
                halo_copy(later, 0).start()

            @pl.when(has_left)
            def _():
                halo_copy(later, 1).start()

            other[:, columns(h)] = t_next
        out[:, columns(h)] += coef[k + 1] * t_next

    for k in range(ITERS):
        if k == 1:
            gather_blocks()
        for h in range(streams):
            part_stage(k, h)
        for h in range(streams):
            finish_stage(k, h)

    steps(1, 4, lambda j: block_copy(j).wait_send())
    for q in range(ITERS * streams):
        if q >= streams:
            steps(1, pairs, lambda j: moment_copy(q, j).wait_send())

            @pl.when(has_right)
            def _():
                halo_copy(q, 0).wait_send()

            @pl.when(has_left)
            def _():
                halo_copy(q, 1).wait_send()

            steps(1, 4, lambda j: part_copy(q, j).wait_send())
        else:
            mate_part(q).wait_send()


def shards(probes, cheb_coef, col_basis, row_basis, near_tiles, coupling, far_rows, far_cols):
    leaf_count, rank = coupling.shape[0], coupling.shape[1]
    rows, width = probes.shape
    count = lax.axis_size("blocks")
    chips, pairs = count // 2, count // 4
    cap = 2 * leaf_count // count
    depth = -(-2 * cap // 16) * 16
    ids = far_rows[:, 0]
    order = jnp.arange(leaf_count, dtype=jnp.int32)
    earlier = (ids[None, :] == ids[:, None]) & (order[None, :] < order[:, None])
    nth = jnp.sum(earlier.astype(jnp.int32), axis=1)
    slot = (ids // 2) * depth + (ids % 2) * cap + nth
    place = (slot[None, :] == jnp.arange(chips * depth, dtype=jnp.int32)[:, None]).astype(jnp.bfloat16)
    tag_width = -(-2 * count // 128) * 128
    tag = (ids % 2) * count + far_cols
    tags = (tag[:, None] == jnp.arange(tag_width, dtype=jnp.int32)[None, :]).astype(jnp.bfloat16)
    flat = jnp.concatenate([coupling.reshape(leaf_count, rank * rank), tags], axis=1)
    sent = jnp.dot(place, flat, preferred_element_type=jnp.float32).astype(jnp.bfloat16)
    sent = sent.reshape(chips, depth, flat.shape[1])

    vmem = pl.BlockSpec(memory_space=pltpu.VMEM)
    dma = pltpu.SemaphoreType.DMA
    lanes = LANES
    turns = ITERS * (width // lanes)
    grant = 48 * 1024 * 1024
    got, moments_0, near_0, basis_t = pl.pallas_call(
        functools.partial(start_kernel, count),
        out_shape=[
            jax.ShapeDtypeStruct(sent.shape, jnp.bfloat16),
            jax.ShapeDtypeStruct((2, 2, pairs, rank, width), jnp.bfloat16),
            jax.ShapeDtypeStruct((rows, width), jnp.float32),
            jax.ShapeDtypeStruct((rank, rows), jnp.bfloat16),
        ],
        in_specs=[vmem] * 4,
        out_specs=[vmem] * 4,
        scratch_shapes=[
            pltpu.VMEM((2, rows, width), jnp.bfloat16),
            dma((chips,)), dma((chips,)), dma((chips,)), dma((chips,)), dma((2,)), dma((2,)), dma((2,)),
        ],
        compiler_params=pltpu.CompilerParams(
            collective_id=0, has_side_effects=True, vmem_limit_bytes=grant
        ),
    )(probes, col_basis, near_tiles, sent)

    got = got.reshape(chips * depth, flat.shape[1])
    mine = lax.dot_general(
        got[:, rank * rank : rank * rank + 2 * count], got[:, : rank * rank],
        (((0,), (0,)), ((), ())), preferred_element_type=jnp.float32,
    ).astype(jnp.bfloat16)
    pieces = mine.reshape(2, pairs, 4, rank, rank).transpose(2, 0, 3, 1, 4)
    pieces = pieces.reshape(4, 2 * rank, pairs * rank)

    return pl.pallas_call(
        functools.partial(chebyshev_kernel, count),
        out_shape=jax.ShapeDtypeStruct((rows, width), jnp.float32),
        in_specs=[pl.BlockSpec(memory_space=pltpu.SMEM)] + [vmem] * 7,
        out_specs=vmem,
        scratch_shapes=[
            pltpu.VMEM((turns, pairs, rank, lanes), jnp.bfloat16),
            pltpu.VMEM((turns, 2, rows, lanes), jnp.bfloat16),
            pltpu.VMEM((turns, rows, lanes), jnp.bfloat16),
            pltpu.VMEM((4, 2 * rank, pairs * rank), jnp.bfloat16),
            pltpu.VMEM((4 * rank, pairs * rank), jnp.bfloat16),
            pltpu.VMEM((turns, 4, rank, lanes), jnp.bfloat16),
            pltpu.VMEM((turns, 4, rank, lanes), jnp.bfloat16),
            pltpu.VMEM((rows, width), jnp.float32),
            pltpu.VMEM((rows, width), jnp.float32),
            pltpu.VMEM((rows, width), jnp.float32),
            dma((turns, pairs)), dma((turns, pairs)), dma((turns, 2)), dma((turns, 2)),
            dma((turns, 4)), dma((turns, 4)), dma((4,)), dma((4,)),
        ],
        compiler_params=pltpu.CompilerParams(
            collective_id=1, has_side_effects=True, vmem_limit_bytes=grant
        ),
    )(cheb_coef, probes, basis_t, row_basis, near_tiles, pieces, moments_0, near_0)


def solution(mesh):
    return jax.shard_map(
        shards,
        mesh=mesh,
        in_specs=(
            P(("groups", "blocks"), None),
            P("groups"),
            P(("groups", "blocks"), None),
            P(("groups", "blocks"), None),
            P(("groups", "blocks"), None),
            P(("groups", "blocks"), None, None),
            P(("groups", "blocks"), None),
            P(("groups", "blocks")),
        ),
        out_specs=P(("groups", "blocks"), None),
        check_vma=False,
    )
```

time: 77.7 us -> 73.5 us (0.946)
  Pallas kernels: 70.2 us -> 66 us
    pallas_call x1, Pallas kernels: 34.4 us -> 28.2 us  [shards(): pl.pallas_call(functools.partial(start_kernel, count), out_shape=[jax.Sha...]
    pallas_call x1, Pallas kernels: 35.8 us -> 37.8 us  [shards(): pl.pallas_call(functools.partial(chebyshev_kernel, count), out_shape=jax....]
where the time goes in v3:
time: 73.5 us; the launch traced here: 73.3 us
  Pallas kernels  66 us (90%)
  local copies, waits for them, and re-layouts  4.78 us (7%)
  other arithmetic  1.67 us (2%)
    pallas_call x1, Pallas kernels, shards(): pl.pallas_call(functools.partial(chebyshev_kernel, count), out_shape=jax....  37.8 us
    pallas_call x1, Pallas kernels, shards(): pl.pallas_call(functools.partial(start_kernel, count), out_shape=[jax.Sha...  28.2 us
    reshape x1, local copies, waits for them, and re-layouts, shards(): coupling.reshape(leaf_count, rank * rank)  2.07 us

profile of v3, /device:TPU:0, one launch (start us, length us, event | category | flops | bytes accessed | tf_op | source)
XLA Modules:
  0.0 73.3 jit_solution(1108684767502726813)
XLA Ops:
  0.0 0.9 %convert_reduce_fusion = s32[64]{0:T(128)S(1)} fusion(s32[64]{0:T(128)} %bitcast.15), kind=kLoop, calls=%fused_computation.11 | loop fusion | flops 20416 | bytes 512 | tf_op jit(solution)/shard_map/reduce_sum | solution.py:390
  0.9 0.7 add_add_fusion
  1.6 0.1 fusion.7
  1.7 2.1 %reshape.71 = bf16[64,4096]{1,0:T(8,128)(2,1)S(1)} reshape(bf16[64,64,64]{2,1,0:T(8,128)(2,1)} %param.13) | data formatting | bytes 1048576 | tf_op jit(solution)/shard_map/reshape | solution.py:396
  3.8 0.0 copy-start.3
  3.8 0.0 copy-start
  3.8 0.0 copy-start.1
  3.8 0.4 convolution_convert_fusion
  4.2 0.3 copy-done.3
  4.5 0.1 copy.12.col_basis
  4.6 0.1 copy-done
  4.8 0.0 copy-done.1
  4.8 28.2 %shard_map.82 = (bf16[8,16,4224]{2,1,0:T(8,128)(2,1)S(1)}, bf16[2,2,4,64,256]{4,3,2,1,0:T(8,128)(2,1)S(1)}, f32[256,256]{1,0:T(8,128)S(1)}, bf16[64,256]{1,0:T(8,128)(2,1)S(1)}) custom-call(bf16[256,256]{1,0:T(8,128)(2,1)S(1)} %copy-done.1, bf16[256,64]{1,0:T(8,128)(2,1)S(1)} %copy.12.col_basis, bf16[256,768]{1,0:T(8,128)(2,1)S(1)} %copy-done, ...), custom_call_target="tpu_custom_call" | custom-call | tf_op jit(solution)/shard_map/pallas_call | solution.py:405
  33.0 0.3 convolution_convert_fusion.1
  33.3 0.5 reshape.74
  33.8 0.0 copy-start.4
  33.8 0.0 copy-start.2
  33.9 0.4 copy.16
  34.3 0.3 reshape.75.pieces
  34.6 0.0 copy-done.4
  34.6 0.1 copy.14.row_basis
  34.7 0.0 copy-done.2
  34.8 37.8 %shard_map.83 = f32[256,256]{1,0:T(8,128)S(1)} custom-call(f32[5]{0:T(128)S(1)} %copy-done.2, bf16[256,256]{1,0:T(8,128)(2,1)S(1)} %copy-done.1, bf16[64,256]{1,0:T(8,128)(2,1)S(1)} %get-tuple-element.9.basis_t, bf16[256,64]{1,0:T(8,128)(2,1)S(1)} %copy.14.row_basis, bf16[256,768]{1,0:T(8,128)(2,1)S(1)} %copy-done, bf16[4,128,256]{2,1,0:T(8,128)(2,1)S(1)} %reshape.75.pieces, ...), custom_call_target="tpu_custom_call" | custom-call | tf_op jit(solution)/shard_map/pallas_call | solution.py:432
  72.6 0.7 copy.18
Async XLA Ops:
  3.8 0.8 %copy-start.3 = (bf16[256,64]{0,1:T(8,128)(2,1)S(1)}, bf16[256,64]{0,1:T(8,128)(2,1)}, u32[]{:S(2)}) copy-start(bf16[256,64]{0,1:T(8,128)(2,1)} %param.10) | copy-start | bytes 98308
  3.8 1.0 %copy-start = (bf16[256,768]{1,0:T(8,128)(2,1)S(1)}, bf16[256,768]{1,0:T(8,128)(2,1)}, u32[]{:S(2)}) copy-start(bf16[256,768]{1,0:T(8,128)(2,1)} %near.3) | copy-start | bytes 1179652
  3.8 1.0 %copy-start.1 = (bf16[256,256]{1,0:T(8,128)(2,1)S(1)}, bf16[256,256]{1,0:T(8,128)(2,1)}, u32[]{:S(2)}) copy-start(bf16[256,256]{1,0:T(8,128)(2,1)} %probes.3) | copy-start | bytes 393220
  33.8 0.8 %copy-start.4 = (bf16[256,64]{0,1:T(8,128)(2,1)S(1)}, bf16[256,64]{0,1:T(8,128)(2,1)}, u32[]{:S(2)}) copy-start(bf16[256,64]{0,1:T(8,128)(2,1)} %param.11) | copy-start | bytes 98308
  33.8 0.9 %copy-start.2 = (f32[5]{0:T(128)S(1)}, f32[5]{0:T(128)}, u32[]{:S(2)}) copy-start(f32[5]{0:T(128)} %coef.1) | copy-start | bytes 64

commit v4 on v3

--- a/solution.py
+++ b/solution.py
@@ -107,7 +107,11 @@
         return remote(probes, halo.at[way], halo_send.at[way], halo_recv.at[way], at(target))
 
     steps(1, chips, lambda j: moment_copy(j).start())
-    steps(1, chips, lambda j: slot_copy(j).start())
+    if chips <= 8:
+        for j in sorted(range(1, chips), key=lambda j: abs(2 * j - chips)):
+            slot_copy(j).start()
+    else:
+        steps(1, chips, lambda j: slot_copy(j).start())
 
     @pl.when(has_right)
     def _():

time: 73.5 us -> 73 us (level)
    pallas_call x1, Pallas kernels: 37.8 us -> 34.7 us  [shards(): pl.pallas_call(functools.partial(chebyshev_kernel, count), out_shape=jax....]
    pallas_call x1, Pallas kernels: 28.2 us -> 30.8 us  [shards(): pl.pallas_call(functools.partial(start_kernel, count), out_shape=[jax.Sha...]
where the time goes in v4:
time: 73 us; the launch traced here: 72.8 us
  Pallas kernels  65.5 us (90%)
  local copies, waits for them, and re-layouts  4.78 us (7%)
  other arithmetic  1.67 us (2%)
    pallas_call x1, Pallas kernels, shards(): pl.pallas_call(functools.partial(chebyshev_kernel, count), out_shape=jax....  34.7 us
    pallas_call x1, Pallas kernels, shards(): pl.pallas_call(functools.partial(start_kernel, count), out_shape=[jax.Sha...  30.8 us
    reshape x1, local copies, waits for them, and re-layouts, shards(): coupling.reshape(leaf_count, rank * rank)  2.07 us

profile of v4, /device:TPU:0, one launch (start us, length us, event | category | flops | bytes accessed | tf_op | source)
XLA Modules:
  0.0 72.8 jit_solution(4405539870063982842)
XLA Ops:
  0.0 0.9 %convert_reduce_fusion = s32[64]{0:T(128)S(1)} fusion(s32[64]{0:T(128)} %bitcast.15), kind=kLoop, calls=%fused_computation.11 | loop fusion | flops 20416 | bytes 512 | tf_op jit(solution)/shard_map/reduce_sum | solution.py:394
  0.9 0.7 add_add_fusion
  1.6 0.1 fusion.7
  1.7 2.1 %reshape.71 = bf16[64,4096]{1,0:T(8,128)(2,1)S(1)} reshape(bf16[64,64,64]{2,1,0:T(8,128)(2,1)} %param.13) | data formatting | bytes 1048576 | tf_op jit(solution)/shard_map/reshape | solution.py:400
  3.8 0.0 copy-start.3
  3.8 0.0 copy-start
  3.8 0.0 copy-start.1
  3.8 0.4 convolution_convert_fusion
  4.2 0.3 copy-done.3
  4.5 0.1 copy.12.col_basis
  4.6 0.1 copy-done
  4.8 0.0 copy-done.1
  4.8 30.8 %shard_map.82 = (bf16[8,16,4224]{2,1,0:T(8,128)(2,1)S(1)}, bf16[2,2,4,64,256]{4,3,2,1,0:T(8,128)(2,1)S(1)}, f32[256,256]{1,0:T(8,128)S(1)}, bf16[64,256]{1,0:T(8,128)(2,1)S(1)}) custom-call(bf16[256,256]{1,0:T(8,128)(2,1)S(1)} %copy-done.1, bf16[256,64]{1,0:T(8,128)(2,1)S(1)} %copy.12.col_basis, bf16[256,768]{1,0:T(8,128)(2,1)S(1)} %copy-done, ...), custom_call_target="tpu_custom_call" | custom-call | tf_op jit(solution)/shard_map/pallas_call | solution.py:409
  35.6 0.3 convolution_convert_fusion.1
  35.9 0.5 reshape.74
  36.4 0.0 copy-start.4
  36.5 0.0 copy-start.2
  36.5 0.4 copy.16
  36.9 0.3 reshape.75.pieces
  37.2 0.0 copy-done.4
  37.2 0.1 copy.14.row_basis
  37.4 0.0 copy-done.2
  37.4 34.7 %shard_map.83 = f32[256,256]{1,0:T(8,128)S(1)} custom-call(f32[5]{0:T(128)S(1)} %copy-done.2, bf16[256,256]{1,0:T(8,128)(2,1)S(1)} %copy-done.1, bf16[64,256]{1,0:T(8,128)(2,1)S(1)} %get-tuple-element.9.basis_t, bf16[256,64]{1,0:T(8,128)(2,1)S(1)} %copy.14.row_basis, bf16[256,768]{1,0:T(8,128)(2,1)S(1)} %copy-done, bf16[4,128,256]{2,1,0:T(8,128)(2,1)S(1)} %reshape.75.pieces, ...), custom_call_target="tpu_custom_call" | custom-call | tf_op jit(solution)/shard_map/pallas_call | solution.py:436
  72.0 0.7 copy.18
Async XLA Ops:
  3.8 0.8 %copy-start.3 = (bf16[256,64]{0,1:T(8,128)(2,1)S(1)}, bf16[256,64]{0,1:T(8,128)(2,1)}, u32[]{:S(2)}) copy-start(bf16[256,64]{0,1:T(8,128)(2,1)} %param.10) | copy-start | bytes 98308
  3.8 1.0 %copy-start = (bf16[256,768]{1,0:T(8,128)(2,1)S(1)}, bf16[256,768]{1,0:T(8,128)(2,1)}, u32[]{:S(2)}) copy-start(bf16[256,768]{1,0:T(8,128)(2,1)} %near.3) | copy-start | bytes 1179652
  3.8 1.0 %copy-start.1 = (bf16[256,256]{1,0:T(8,128)(2,1)S(1)}, bf16[256,256]{1,0:T(8,128)(2,1)}, u32[]{:S(2)}) copy-start(bf16[256,256]{1,0:T(8,128)(2,1)} %probes.3) | copy-start | bytes 393220
  36.4 0.8 %copy-start.4 = (bf16[256,64]{0,1:T(8,128)(2,1)S(1)}, bf16[256,64]{0,1:T(8,128)(2,1)}, u32[]{:S(2)}) copy-start(bf16[256,64]{0,1:T(8,128)(2,1)} %param.11) | copy-start | bytes 98308
  36.5 0.9 %copy-start.2 = (f32[5]{0:T(128)S(1)}, f32[5]{0:T(128)}, u32[]{:S(2)}) copy-start(f32[5]{0:T(128)} %coef.1) | copy-start | bytes 64
